TPU v7x, 256 devices: a whole 4x4x8 slice. The times are simulated.
256 devices in a mesh: expert: 64 (over y, z, core), row: 4 (over x).
Axes of the slice: x: 4, y: 4, z: 8, core: 2. Of those that a mesh axis runs over, the one named last changes fastest.
Arguments:
- tokens: bfloat16 [1024, 7168], P('expert', 'row'), may hold values from -6 to 6
- routes: int32 [1024, 8], P('expert'), may hold values from 0 to 63, all different within a row; in each aligned block of 16 rows (0 to 15, 16 to 31, ...) at most 4 rows name the same one
- probs: float32 [1024, 8], P('expert'), may hold values from 0.02 to 0.3
- gate_weight: bfloat16 [64, 1024, 7168], P('expert', 'row'), may hold values from -0.0625 to 0.0625
- up_weight: bfloat16 [64, 1024, 7168], P('expert', 'row'), may hold values from -0.0625 to 0.0625
- down_weight: bfloat16 [64, 1024, 7168], P('expert', 'row'), may hold values from -0.1875 to 0.1875
- masks: int32 [64, 1024, 128], P('expert', 'row'), may hold values from 0 to 1, as said below
- inv_factor: float32 [128, 128], replicated, as said below
Outputs:
- pruned_panel: bfloat16 [64, 1024, 128], P('expert', 'row')
- moe_out: bfloat16 [1024, 7168], P('expert', 'row')
- hessian: float32 [7168, 7168], P('row', 'expert')
Inputs may be any that keep to these rules, and one draw needn't show every extreme that they name: `routes`: a token's 8 entries name different experts; within the rows of one device (aligned blocks of 16 tokens) no expert is named more than 4 times, a bound that some block reaches. `masks`: in each aligned group of 4 columns of a row exactly 2 entries are 1. `inv_factor`: upper triangular with a positive diagonal.
All inputs are finite; a program needn't handle non-finite values.
Results may differ from a plain program's by a relative error of at most 0.0075.
Values may be sent and summed in bfloat16 or wider, within the bound.
A program may use at most 128 MiB of HBM per device.

v0:
```python
import jax
import jax.numpy as jnp
from jax import lax
from jax.sharding import PartitionSpec as P


def prune_local(gate_local, keep_mask, inv_factor, panel_cols):
    model_width = gate_local.shape[1]
    current = gate_local[:, model_width - panel_cols :].astype(jnp.float32)
    columns = jnp.arange(panel_cols, dtype=jnp.int32)

    def block_step(block_idx, current):
        offset = block_idx * 16
        segment = lax.dynamic_slice_in_dim(current, offset, 16, 1)
        keep_seg = lax.dynamic_slice_in_dim(keep_mask, offset, 16, 1)
        factor_rows = lax.dynamic_slice_in_dim(inv_factor, offset, 16, 0)
        inner_block = lax.dynamic_slice_in_dim(factor_rows, offset, 16, 1)
        error_list = []
        for column_idx in range(16):
            column = segment[:, column_idx]
            kept_vals = column * keep_seg[:, column_idx]
            errors_now = (column - kept_vals) / inner_block[column_idx, column_idx]
            segment = segment - errors_now[:, None] * inner_block[column_idx][None, :]
            segment = segment.at[:, column_idx].set(kept_vals)
            error_list.append(errors_now)
        errors_all = jnp.stack(error_list, axis=1)
        update = jnp.dot(errors_all, factor_rows, precision=lax.Precision.HIGHEST)
        later = (columns >= offset + 16)[None, :]
        current = current - jnp.where(later, update, 0.0)
        return lax.dynamic_update_slice_in_dim(current, segment, offset, 1)

    return lax.fori_loop(0, panel_cols // 16, block_step, current).astype(jnp.bfloat16)


def on_device(tokens, routes, probs, gate_weight, up_weight, down_weight, masks, inv_factor):
    expert_count = lax.axis_size("expert")
    row_count = lax.axis_size("row")
    token_count = routes.shape[0]
    top_count = routes.shape[1]
    capacity = min(token_count, max(2, 2 * token_count * top_count // expert_count))
    model_width = gate_weight.shape[2]
    panel_cols = masks.shape[2]
    slot_total = expert_count * capacity
    row_idx = lax.axis_index("row")
    expert_idx = lax.axis_index("expert")
    row_block = model_width // row_count
    pruned = prune_local(gate_weight[0], masks[0].astype(jnp.float32), inv_factor, panel_cols)
    flat_ids = routes.reshape(-1)
    onehot = (flat_ids[:, None] == jnp.arange(expert_count, dtype=jnp.int32)[None, :]).astype(
        jnp.int32
    )
    slot_index = jnp.sum((jnp.cumsum(onehot, axis=0) - onehot) * onehot, axis=1)
    target = flat_ids * capacity + slot_index
    chosen = target[:, None] == jnp.arange(slot_total, dtype=jnp.int32)[None, :]
    dispatch_mat = jnp.sum(
        chosen.astype(jnp.float32).reshape(token_count, top_count, slot_total), axis=1
    ).T
    combine_mat = jnp.sum(
        jnp.where(chosen, probs.reshape(-1)[:, None], 0.0).reshape(
            token_count, top_count, slot_total
        ),
        axis=1,
    )
    dispatch_bf = dispatch_mat.astype(jnp.bfloat16)
    full_tokens = lax.all_gather(tokens, "row", axis=1, tiled=True)
    outgoing = jnp.dot(dispatch_bf, full_tokens, preferred_element_type=jnp.float32).astype(
        jnp.bfloat16
    )
    arrived = lax.all_to_all(
        outgoing.reshape(expert_count, capacity, model_width),
        "expert",
        split_axis=0,
        concat_axis=0,
        tiled=True,
    )
    arrived_rows = arrived.reshape(slot_total, model_width)
    contract = (((1,), (1,)), ((), ()))
    split_at = model_width - panel_cols
    gate_val = lax.dot_general(
        arrived_rows[:, :split_at],
        gate_weight[0, :, :split_at],
        contract,
        preferred_element_type=jnp.float32,
    )
    gate_val = gate_val + lax.dot_general(
        arrived_rows[:, split_at:], pruned, contract, preferred_element_type=jnp.float32
    )
    up_val = lax.dot_general(
        arrived_rows, up_weight[0], contract, preferred_element_type=jnp.float32
    )
    hidden = (jax.nn.silu(gate_val) * up_val).astype(jnp.bfloat16)
    down_local = down_weight[0]
    summed = lax.psum_scatter(
        lax.dot_general(
            down_local, hidden, (((0,), (1,)), ((), ())), preferred_element_type=jnp.float32
        ),
        "row",
        scatter_dimension=0,
        tiled=True,
    )
    feature_cols = summed.shape[0]
    expert_outputs = summed.astype(jnp.bfloat16).reshape(feature_cols, expert_count, capacity)
    returned = lax.all_to_all(expert_outputs, "expert", split_axis=1, concat_axis=1, tiled=True)
    returned_flat = returned.reshape(feature_cols, slot_total).astype(jnp.float32)
    moe_local = lax.dot_general(
        combine_mat, returned_flat, contract, precision=lax.Precision.HIGHEST
    ).astype(jnp.bfloat16)
    total_tokens = token_count * expert_count
    block_cols = model_width // expert_count
    tokens_first = (((0,), (0,)), ((), ()))
    full_outputs = lax.all_gather(moe_local, "row", axis=1, tiled=True)
    segment = lax.all_gather(full_outputs, "expert", axis=0, tiled=True)
    left_cols = lax.dynamic_slice_in_dim(segment, row_idx * row_block, row_block, 1)
    right_cols = lax.dynamic_slice_in_dim(segment, expert_idx * block_cols, block_cols, 1)
    hess_block = lax.dot_general(
        left_cols, right_cols, tokens_first, preferred_element_type=jnp.float32
    )
    hessian = hess_block * (2.0 / total_tokens)
    return (pruned[None], moe_local, hessian)


def solution(mesh):
    in_specs = (
        P("expert", "row"),
        P("expert", None),
        P("expert", None),
        P("expert", "row", None),
        P("expert", "row", None),
        P("expert", "row", None),
        P("expert", "row", None),
        P(),
    )
    out_specs = (P("expert", "row", None), P("expert", "row"), P("row", "expert"))
    return jax.shard_map(
        on_device, mesh=mesh, in_specs=in_specs, out_specs=out_specs, check_vma=False
    )
```

profile of v0, /device:TPU:1, one launch (start us, length us, event | category | flops | bytes accessed | tf_op | source)
XLA Modules:
  0.0 663.0 jit_solution(38209603336617948)
XLA Ops:
  9.3 10.8 %all_gather.9 = bf16[16,7168]{1,0:T(8,128)(2,1)S(1)} all-gather(bf16[16,1792]{1,0:T(8,128)(2,1)} %param.42), channel_id=1, replica_groups=mesh['expert'=64,'row'=4] {'row'}, dimensions={1}, use_global_device_ids=true | all-gather | bytes 286720 | tf_op jit(solution)/shard_map/all_gather | solution.py:65
  20.2 2.9 convolution_convert_fusion
  23.2 7.0 %reshape.798 = bf16[64,4,7168]{2,1,0:T(4,128)(2,1)} reshape(bf16[256,7168]{1,0:T(8,128)(2,1)} %convolution_convert_fusion) | data formatting | bytes 7340032 | tf_op jit(solution)/shard_map/reshape | solution.py:70
  30.2 15.4 %all-to-all-start = ((bf16[64,4,7168]{2,1,0:T(4,128)(2,1)}), bf16[64,4,7168]{2,1,0:T(4,128)(2,1)}, u32[]{:S(2)}, u32[]{:S(2)}) async-start(bf16[64,4,7168]{2,1,0:T(4,128)(2,1)} %reshape.798), calls=%async_computation | async-start | bytes 7340032 | tf_op jit(solution)/shard_map/all_to_all | solution.py:69
  52.0 359.1 %while.34 = (s32[]{:T(128)}, f32[256,128]{1,0:T(8,128)S(1)}, f32[256,128]{1,0:T(8,128)S(1)}, f32[128,128]{1,0:T(8,128)}, pred[]{:T(512)}, /*index=5*/pred[]{:T(5...) while((s32[]{:T(128)}, f32[256,128]{1,0:T(8,128)S(1)}, ...), condition=%wide.region_17.18_spmd.clone, body=%wide.region_15.17_spmd.clone.sunk | while | flops 6508715 | bytes 1094288 | solution.py:32
  54.0 1.8 fusion.83
  98.7 1.8 fusion.83
  138.3 1.1 fusion.100
  143.6 1.8 fusion.83
  183.2 1.1 fusion.100
  188.5 1.8 fusion.83
  233.3 1.8 fusion.83
  278.2 1.8 fusion.83
  323.1 1.8 fusion.83
  368.0 1.8 fusion.83
  411.1 6.7 %reshape.799 = bf16[256,7168]{1,0:T(8,128)(2,1)} reshape(bf16[64,4,7168]{2,1,0:T(4,128)(2,1)} %all-to-all-done) | data formatting | bytes 7340032 | tf_op jit(solution)/shard_map/reshape | solution.py:76
  417.9 4.3 fusion.10
  423.2 11.2 %convolution_bitcast_fusion = f32[7168,256]{0,1:T(8,128)} fusion(bf16[1,256,7168]{2,1,0:T(8,128)(2,1)} %param.47, bf16[256,7168]{1,0:T(8,128)(2,1)} %reshape.799, bf16[1,256,7168]{2,1,0:T(8,128)(2,1)} %param.46, f32[256,256]{1,0:T(8,128)S(1)} %convolution_add_fusion), kind=kOutput, calls=%fused_computation.87 | convolution fusion | flops 1879441408 | bytes 18612224 | tf_op jit(solution)/shard_map/dot_general | solution.py:94
  434.5 75.5 %reduce-scatter.2.cloned.1.call-done = f32[1792,256]{0,1:T(8,128)} async-done(((f32[7168,256]{0,1:T(8,128)}), f32[1792,256]{0,1:T(8,128)}) %reduce-scatter.2.cloned.1.call-update) | async-done | bytes 1835024 | tf_op jit(solution)/shard_map/reduce_scatter | solution.py:93
  510.0 1.6 convert_element_type.45
  511.8 36.2 %all_to_all.10 = bf16[1792,64,4]{0,2,1:T(4,128)(2,1)S(1)} all-to-all(bf16[1792,64,4]{0,2,1:T(4,128)(2,1)S(1)} %reshape.800), channel_id=1, replica_groups=mesh['expert'=64,'row'=4] {'expert'}, dimensions={1} | all-to-all | bytes 1835008 | tf_op jit(solution)/shard_map/all_to_all | solution.py:103
  548.7 10.0 %all_gather.10 = bf16[16,7168]{1,0:T(8,128)(2,1)} all-gather(bf16[16,1792]{1,0:T(8,128)(2,1)S(1)} %convolution_convert_fusion.1), channel_id=1, replica_groups=mesh['expert'=64,'row'=4] {'row'}, dimensions={1}, use_global_device_ids=true | all-gather | bytes 286720 | tf_op jit(solution)/shard_map/all_gather | solution.py:111
  559.4 92.9 %all-gather.2.cloned.1.call-done = bf16[1024,7168]{1,0:T(8,128)(2,1)} async-done(((bf16[16,7168]{1,0:T(8,128)(2,1)}), bf16[1024,7168]{1,0:T(8,128)(2,1)}) %all-gather.2.cloned.1.call-update) | async-done | bytes 14680080 | tf_op jit(solution)/shard_map/all_gather | solution.py:112
  652.3 3.8 fusion.14
  (719 shorter events, 350.4 us)
Async XLA Ops:
  30.2 21.0 %copy-start.1 = (s32[1,256,128]{2,1,0:T(8,128)S(1)}, s32[1,256,128]{2,1,0:T(8,128)}, u32[]{:S(2)}) copy-start(s32[1,256,128]{2,1,0:T(8,128)} %param.48) | copy-start | bytes 393220
  30.2 380.9 %all-to-all-start = ((bf16[64,4,7168]{2,1,0:T(4,128)(2,1)}), bf16[64,4,7168]{2,1,0:T(4,128)(2,1)}, u32[]{:S(2)}, u32[]{:S(2)}) async-start(bf16[64,4,7168]{2,1,0:T(4,128)(2,1)} %reshape.798), calls=%async_computation | async-start | bytes 7340032 | tf_op jit(solution)/shard_map/all_to_all | solution.py:69
  45.6 464.4 %reduce-scatter.2.cloned.1.call-start = ((), (), s32[]{:S(2)}) async-start(), calls=%async_computation.3 | async-start | bytes 9175040 | tf_op jit(solution)/shard_map/reduce_scatter | solution.py:93
  434.4 217.9 %all-gather.2.cloned.1.call-start = ((), (), s32[]{:S(2)}) async-start(), calls=%async_computation.4 | async-start | bytes 14909440 | tf_op jit(solution)/shard_map/all_gather | solution.py:112
  548.7 107.4 %copy-start = (bf16[16,1792]{1,0:T(8,128)(2,1)}, bf16[16,1792]{1,0:T(8,128)(2,1)S(1)}, u32[]{:S(2)}) copy-start(bf16[16,1792]{1,0:T(8,128)(2,1)S(1)} %convolution_convert_fusion.1) | copy-start | bytes 172036
Sparse Core Ops, SparseCore 0:
  434.5 75.4 reduce-scatter.1
  558.9 93.3 all-gather.1
where the time goes:
time: 667 us; the launch traced here: 663 us
  other arithmetic  239 us (36%)
  waiting for transfers between devices  168 us (25%)
  local copies, waits for them, and re-layouts  133 us (20%)
  blocking collectives  57 us (9%)
  matrix products  32.5 us (5%)
  starting transfers between devices  15.5 us (2%)
  between operations  14.1 us (2%)
    another operation x144, other arithmetic  113 us
    div x128, other arithmetic, block_step(): errors_now = (column - kept_vals) / inner_block[column_idx, column_idx]  108 us
    all_gather x1, waiting for transfers between devices, on_device(): segment = lax.all_gather(full_outputs, 'expert', axis=0, tiled=True)  92.9 us
    scatter x128, local copies, waits for them, and re-layouts, block_step(): segment = segment.at[:, column_idx].set(kept_vals)  77 us
    reduce_scatter x1, waiting for transfers between devices, on_device(): lax.psum_scatter(lax.dot_general(down_local, hidden, (((0,), (1,)), ((),...  75.5 us
    all_to_all x1, blocking collectives, on_device(): lax.all_to_all(expert_outputs, 'expert', split_axis=1, concat_axis=1, til...  36.2 us
    all_to_all x1, starting transfers between devices, on_device(): lax.all_to_all(outgoing.reshape(expert_count, capacity, model_width), 'ex...  15.4 us
    sub x128, other arithmetic, block_step(): segment = segment - errors_now[:, None] * inner_block[column_idx][None, :]  14.2 us
  transfers between devices with their start and end apart: 3, of which 2 were waited for; matrix products, arithmetic and copies ran while one was open for 55% of the time, Pallas kernels for 0%

commit v1 on v0

v1 whole, which is shorter than its diff:
```python
import functools

import jax
import jax.numpy as jnp
from jax import lax
from jax.experimental import pallas as pl
from jax.experimental.pallas import tpu as pltpu
from jax.sharding import PartitionSpec as P

NX, NY, NZ, NC = 4, 4, 8, 2
TOK = 16
CAP = 4
PANEL = 128
FB = 1792
HALF = FB // 2
INFO = 128
WIDE = INFO + FB
CUTS = ((0, INFO + HALF), (INFO + HALF, HALF))
RET = (1024, FB - 1024)
BASE = (0, RET[0])
WB = 256
WA = RET[1] - WB
SLOTS = CAP * NY * NZ * NC
CH = SLOTS // NY
HID = 256
CT = NZ * NC * TOK
BLK = 112
MESH = pl.DeviceIdType.MESH
F32 = jnp.float32
BF = jnp.bfloat16
COPIES = 240
CONTRACT = (((1,), (1,)), ((), ()))
ZNEAR = (1, 7, 2, 6, 3, 5, 4)
YNEAR = (1, 3)
PLANES = (0, 1, 3, 2)


def wrap(value, n):
    return lax.rem(value + 4 * n, n)


def iota(shape, axis):
    return lax.broadcasted_iota(jnp.int32, shape, axis)


class Net:
    def __init__(self, send, recv):
        self.send, self.recv, self.count, self.pending = send, recv, 0, []

    def make(self, src, dst, dev, recv_index=None):
        index = self.count
        self.count += 1
        return pltpu.make_async_remote_copy(
            src_ref=src,
            dst_ref=dst,
            send_sem=self.send.at[index],
            recv_sem=self.recv.at[index if recv_index is None else recv_index],
            device_id=dev,
            device_id_type=MESH,
        )

    def copy(self, src, dst, dev):
        made = self.make(src, dst, dev)
        made.start()
        self.pending.append(made)
        return made

    def drain(self):
        for made in self.pending:
            made.wait_send()


def body(
    tokens, routes, probs, gate, up, down, masks, factor,
    pruned_out, moe_out, hess_out,
    gate_v, up_v, down_v, got, rows, sel, slot_prob, part, turn, land,
    spread, sib, ysend, yland, own, zsend, zland,
    full, unit, right, acc, w_t, drop_t, v_t, err_t, wsem, send, recv,
):
    expert = lax.axis_index("expert")
    x = lax.axis_index("row")
    y, z, c = expert // (NZ * NC), (expert // NC) % NZ, expert % NC
    d = 1 - 2 * c
    net = Net(send, recv)

    def at_y(k):
        return ((wrap(y + k, NY) * NZ + z) * NC + c, x)

    def at_z(k):
        return ((y * NZ + wrap(z + k, NZ)) * NC + c, x)

    def at_x(k):
        return (expert, wrap(x + k, NX))

    sibling = (expert + d, x)

    barrier = pltpu.get_barrier_semaphore()
    near = [sibling]
    near += [at_y(k) for k in range(1, NY)]
    near += [at_z(k) for k in range(1, NZ)]
    near += [at_x(k) for k in range(1, NX)]
    for device in near:
        pl.semaphore_signal(barrier, inc=1, device_id=device, device_id_type=MESH)

    weights = {}
    for number, (src, dst) in enumerate(((gate, gate_v), (up, up_v), (down, down_v))):
        for at in (3, 0, 1, 2):
            made = pltpu.make_async_copy(
                src.at[:, pl.ds(at * FB, FB)], dst.at[at], wsem.at[number * NX + at]
            )
            made.start()
            weights[number, at] = made

    lane = iota((INFO, TOK), 0)
    dense = jnp.zeros((INFO, TOK), F32)
    for k in range(routes.shape[0]):
        dense = dense + jnp.where(routes[k : k + 1, :] == lane % 64, probs[k : k + 1, :], 0.0)
    high = dense.astype(BF).astype(F32)
    info = jnp.where(lane < 64, high, dense - high)
    got[y, z, c, :, :INFO] = info.T.astype(BF)
    got[y, z, c, :, INFO:] = tokens[...]

    pl.semaphore_wait(barrier, len(near))

    def prune():
        weights[0, 3].wait()
        w_t[...] = gate_v[3, :, FB - PANEL :].astype(F32).T
        drop_t[...] = (1 - masks[...]).astype(F32).T
        eye = iota((PANEL, PANEL), 0) == iota((PANEL, PANEL), 1)
        upper = factor[...]
        diagonal = jnp.sum(jnp.where(eye, upper, 0.0), axis=1, keepdims=True)
        v_t[...] = (upper / diagonal).T
        err_t[...] = jnp.zeros_like(err_t)
        yield
        for block in range(PANEL // 16):
            lo, hi = block * 16, block * 16 + 16
            seg = w_t[lo:hi, :]
            if block:
                seg = seg - jnp.dot(
                    v_t[lo:hi, :], err_t[...], precision=lax.Precision.HIGHEST, preferred_element_type=F32
                )
            near_t = v_t[lo:hi, lo:hi]
            drop = drop_t[lo:hi, :]
            errors = []
            for i in range(16):
                error = seg[i : i + 1, :] * drop[i : i + 1, :]
                errors.append(error)
                seg = seg - near_t[:, i : i + 1] * error
            err_t[lo:hi, :] = jnp.concatenate(errors, axis=0)
            w_t[lo:hi, :] = seg * (1.0 - drop)
            yield
        result = w_t[...].T.astype(BF)
        pruned_out[...] = result
        gate_v[3, :, FB - PANEL :] = result
        at = iota((PANEL, FB), 1) - (z * NC + c) * BLK
        unit[...] = jnp.where((at == iota((PANEL, FB), 0)) & (at < BLK), 1.0, 0.0).astype(BF)

    pruning = prune()

    def tick(times):
        for _ in range(times):
            next(pruning, None)

    def cut(ref, h):
        return ref.at[:, pl.ds(CUTS[h][0], CUTS[h][1])]

    along_z, along_y, shared = {}, {}, {}
    for h in range(2):
        block = cut(got.at[y, z, c], h)
        for k in ZNEAR:
            along_z[h, k] = net.copy(block, block, at_z(k))
        for m in YNEAR:
            along_y[h, 0, m] = net.copy(block, block, at_y(m))
    tick(3)

    before = (iota((CT, CT), 0) // TOK == iota((CT, CT), 1) // TOK) & (iota((CT, CT), 0) < iota((CT, CT), 1))
    before = before.astype(F32).astype(BF)
    slot_i, tok_i = iota((CH, CT), 0), iota((CH, CT), 1)
    pick = iota((8, INFO), 1)
    pick = jnp.where((pick == expert) | (pick == expert + 64), 1.0, 0.0).astype(BF)

    def choose(j):
        prob = lax.dot_general(
            pick, got[j, :, :, :, :INFO].reshape(CT, INFO), CONTRACT, preferred_element_type=F32
        )
        rank = jnp.dot((prob > 0.0).astype(F32).astype(BF), before, preferred_element_type=F32)
        chosen = (
            (slot_i // CAP == tok_i // TOK)
            & (rank[0:1, :] == (slot_i % CAP).astype(F32))
            & (prob[0:1, :] > 0.0)
        )
        chosen = jnp.where(chosen, 1.0, 0.0)
        slot_prob[j] = jnp.sum(chosen * prob[0:1, :], axis=1, keepdims=True)
        sel[j] = chosen

    ring = {}

    def launch(m, h):
        j = wrap(y - m, NY)
        shared[m, h].wait_recv()
        if h == 0:
            choose(j)
        start, width = CUTS[h][0] + (INFO if h == 0 else 0), HALF
        rows[x, h, j] = jnp.dot(
            sel[j].astype(BF),
            got[j, :, :, :, start : start + width].reshape(CT, width),
            preferred_element_type=F32,
        ).astype(BF)
        block = rows.at[x, h, j]
        ring[m, h, 0] = net.copy(block, block, at_x(d))
        ring[m, h, 1] = net.copy(block, block, at_x(-d))

    def relay(m, h):
        j = wrap(y - m, NY)
        ring[m, h, 0].wait_recv()
        block = rows.at[wrap(x - d, NX), h, j]
        ring[m, h, 2] = net.copy(block, block, at_x(d))

    def share(m, h):
        ref = got.at[wrap(y - m, NY), :, c, :, pl.ds(CUTS[h][0], CUTS[h][1])]
        shared[m, h] = net.copy(ref, ref, sibling)

    def forward(h, ks):
        for k in ks:
            along_z[h, k].wait_recv()
            block = cut(got.at[y, wrap(z - k, NZ), c], h)
            for m in YNEAR:
                along_y[h, k, m] = net.copy(block, block, at_y(m))

    def arrive(m, h):
        for k in (0,) + ZNEAR if m != 2 else (0,):
            along_y[h, k, m].wait_recv()
        if m == (1, 3)[h]:
            ref = got.at[wrap(y - m, NY), :, c, :, pl.ds(CUTS[h][0], CUTS[h][1])]
            along_y[h, 0, 2] = net.copy(ref, ref, at_y(m))
        share(m, h)

    forward(0, ZNEAR)
    share(0, 0)
    tick(1)
    forward(1, ZNEAR[:2])
    launch(0, 0)
    forward(1, ZNEAR[2:])
    share(0, 1)
    tick(1)
    launch(0, 1)
    relay(0, 0)
    order = [(0, 0), (0, 1), (1, 0), (3, 0), (3, 1), (1, 1), (2, 0), (2, 1)]
    arrive(*order[2])
    for n in range(2, len(order)):
        tick(1)
        if n < len(order) - 1:
            arrive(*order[n + 1])
        launch(*order[n])
        relay(*order[n - 1])
    relay(*order[-1])
    tick(16)

    for key in sorted(weights):
        if key != (0, 3):
            weights[key].wait()

    def project(o, h):
        block = rows[o, h].reshape(SLOTS, HALF)
        at = slice(h * HALF, (h + 1) * HALF)
        return (
            lax.dot_general(block, gate_v[o, :, at], CONTRACT, preferred_element_type=F32),
            lax.dot_general(block, up_v[o, :, at], CONTRACT, preferred_element_type=F32),
        )

    gate_val, up_val = project(x, 0)
    for hop, o in ((None, x), (1, wrap(x + d, NX)), (0, wrap(x - d, NX)), (2, wrap(x + 2, NX))):
        for h in range(2):
            if hop is None and h == 0:
                continue
            if hop in (1, 2):
                for m in PLANES:
                    ring[m, h, hop].wait_recv()
            more = project(o, h)
            gate_val, up_val = gate_val + more[0], up_val + more[1]
    hidden = (gate_val / (1.0 + jnp.exp(-gate_val)) * up_val).astype(BF)

    def partial(o):
        part[o] = jnp.dot(hidden, down_v[o], preferred_element_type=F32).astype(BF).reshape(NY, CH, FB)

    steps = (2, 1, 3, 0)
    planes = [wrap(y + k, NY) for k in steps]
    sums, back, along, across = {}, {}, {}, {}

    def place(n):
        h = n // NY
        return planes[n % NY], pl.ds(BASE[h], RET[h]), pl.ds(0, RET[h])

    def first(n):
        j, at, to = place(n)
        sums[n, 0] = net.copy(part.at[wrap(x + 2, NX), j, :, at], land.at[n, 0, :, to], at_x(d))

    def other(n):
        j, at, to = place(n)
        sums[n, 1] = net.copy(part.at[wrap(x - d, NX), j, :, at], land.at[n, 1, :, to], at_x(-d))

    def second(n):
        j, at, to = place(n)
        sums[n, 0].wait_recv()
        turn[n, :, to] = (land[n, 0, :, to].astype(F32) + part[wrap(x + d, NX), j, :, at].astype(F32)).astype(BF)
        sums[n, 2] = net.copy(turn.at[n, :, to], land.at[n, 2, :, to], at_x(d))

    def finish(n):
        j, at, to = place(n)
        sums[n, 1].wait_recv()
        sums[n, 2].wait_recv()
        total = part[x, j, :, at].astype(F32) + land[n, 1, :, to].astype(F32) + land[n, 2, :, to].astype(F32)
        scaled = (total * slot_prob[j]).astype(BF)
        spread[n, :, :, :, to] = (
            jnp.dot(sel[j].T.astype(BF), scaled, preferred_element_type=F32)
            .astype(BF)
            .reshape(NZ, NC, TOK, RET[n // NY])
        )
        back[n] = net.copy(spread.at[n, :, 1 - c, :, to], sib.at[n, :, :, to], sibling)

    def onward(n):
        back[n].wait_recv()
        h, k = n // NY, n % NY
        to = pl.ds(0, RET[h])
        total = spread[n, :, c, :, to].astype(F32) + sib[n, :, :, to].astype(F32)
        if k < NY - 1:
            slot = h * (NY - 1) + k
            ysend[slot, :, :, to] = total.astype(BF)
            along[h, k] = net.copy(ysend.at[slot, :, :, to], yland.at[slot, :, :, to], at_y(steps[k]))
        else:
            own[h, :, :, to] = total

    def whole(h, i):
        to = pl.ds(0, RET[h])
        total = own[h, i, :, to]
        for k in range(NY - 1):
            total = total + yland[h * (NY - 1) + k, i, :, to].astype(F32)
        return total

    def cross(h):
        for k in range(NY - 1):
            along[h, k].wait_recv()
        for k in ZNEAR:
            slot = h * (NZ - 1) + k - 1
            to = pl.ds(0, RET[h])
            zsend[slot, :, to] = whole(h, wrap(z + k, NZ)).astype(BF)
            across[h, k] = net.copy(zsend.at[slot, :, to], zland.at[slot, :, to], at_z(k))

    def settle(h):
        result = whole(h, z)
        for k in ZNEAR:
            across[h, k].wait_recv()
            result = result + zland[h * (NZ - 1) + k - 1, :, pl.ds(0, RET[h])].astype(F32)
        result = result.astype(BF)
        moe_out[:, pl.ds(BASE[h], RET[h])] = result
        full[y, z, c, :, pl.ds(BASE[h], RET[h])] = result

    cuts = (pl.ds(0, RET[0]), pl.ds(RET[0], WA))
    tail = pl.ds(RET[0] + WA, WB)
    az, ay, by, bz, sa = {}, {}, {}, {}, {}

    def spread_z(h):
        ref = full.at[y, z, c, :, cuts[h]]
        for k in ZNEAR:
            az[h, k] = net.copy(ref, ref, at_z(k))
        for m in YNEAR:
            ay[h, 0, m] = net.copy(ref, ref, at_y(m))

    def spread_y(h, ks):
        for k in ks:
            az[h, k].wait_recv()
            ref = full.at[y, wrap(z - k, NZ), c, :, cuts[h]]
            for m in YNEAR:
                ay[h, k, m] = net.copy(ref, ref, at_y(m))

    def draw(j, h):
        at = pl.ds(BASE[h], RET[h])
        more = lax.dot_general(
            unit[:, at], full[j, :, :, :, at].reshape(CT, RET[h]), CONTRACT, preferred_element_type=F32
        ).astype(BF)
        right[j] = more if h == 0 else right[j] + more

    def share_own(h):
        ref = full.at[y, :, c, :, cuts[h]]
        sa[h, 0] = net.copy(ref, ref, sibling)

    def collect(h, m):
        for k in (0,) + ZNEAR if m != 2 else (0,):
            ay[h, k, m].wait_recv()
        ref = full.at[wrap(y - m, NY), :, c, :, cuts[h]]
        if m == (1, 3)[h]:
            ay[h, 0, 2] = net.copy(ref, ref, at_y(m))
        sa[h, m] = net.copy(ref, ref, sibling)

    partial(wrap(x + 2, NX))
    for n in range(3):
        first(n)
    partial(wrap(x - d, NX))
    for n in range(3):
        other(n)
    partial(wrap(x + d, NX))
    partial(x)
    for n in range(2 * NY):
        second(n)
        if n + 3 < 2 * NY:
            first(n + 3)
            other(n + 3)
        if n >= 1:
            finish(n - 1)
        if n >= 2:
            onward(n - 2)
    cross(0)
    finish(7)
    onward(6)
    onward(7)
    settle(0)
    spread_z(0)
    cross(1)
    spread_y(0, ZNEAR)
    share_own(0)
    settle(1)
    ref = full.at[y, z, c, :, tail]
    for m in (1, 2, 3):
        by[m] = net.copy(ref, ref, at_y(m))
    spread_z(1)
    spread_y(1, ZNEAR[:2])
    for m in (1, 2, 3):
        by[m].wait_recv()
    ref = full.at[:, z, c, :, tail]
    for k in ZNEAR:
        bz[k] = net.copy(ref, ref, at_z(k))
    spread_y(1, ZNEAR[2:])
    share_own(1)
    for m in PLANES:
        if m:
            collect(0, m)
        sa[0, m].wait_recv()
        pl.when(x == y)(functools.partial(draw, wrap(y - m, NY), 0))
    for k in ZNEAR:
        bz[k].wait_recv()
    ref = full.at[:, :, c, :, tail]
    sb = net.copy(ref, ref, sibling)
    sb.wait_recv()

    scale = 2.0 / (TOK * NY * NZ * NC)
    cols = {}

    def product(n):
        j = wrap(y - PLANES[n], NY)

        @pl.when(x != y)
        def _():
            cols[n][0].wait_recv()

        for at in range(0, FB, 256):
            more = jnp.dot(
                right[j], full[j, :, :, :, at : at + 256].reshape(CT, 256), preferred_element_type=F32
            )
            if n == 0:
                acc[:, at : at + 256] = more
            elif n < NY - 1:
                acc[:, at : at + 256] += more
            else:
                hess_out[:, at : at + 256] = ((acc[:, at : at + 256] + more) * scale)[:BLK, :]

    for n, m in enumerate(PLANES):
        j = wrap(y - m, NY)
        if m:
            collect(1, m)
        sa[1, m].wait_recv()
        index = net.count
        cols[n] = [net.make(right.at[j], right.at[j], at_x(k), index) for k in (2, 1, 3)]

        @pl.when(x == y)
        def _():
            draw(j, 1)
            for made in cols[n]:
                made.start()

        if n:
            product(n - 1)
    product(NY - 1)

    @pl.when(x == y)
    def _():
        for n in range(NY):
            for made in cols[n]:
                made.wait_send()

    net.drain()


def hand_on(pruned, moe, hessian, pruned_out, moe_out, hess_out):
    pruned_out[...] = pruned[...]
    moe_out[...] = moe[...]
    hess_out[...] = hessian[...]


def on_device(tokens, routes, probs, gate_weight, up_weight, down_weight, masks, inv_factor):
    vmem = pl.BlockSpec(memory_space=pltpu.VMEM)
    hbm = pl.BlockSpec(memory_space=pl.ANY)
    scratch = [
        pltpu.VMEM((NX, HID, FB), BF),
        pltpu.VMEM((NX, HID, FB), BF),
        pltpu.VMEM((NX, HID, FB), BF),
        pltpu.VMEM((NY, NZ, NC, TOK, WIDE), BF),
        pltpu.VMEM((NX, 2, NY, CH, HALF), BF),
        pltpu.VMEM((NY, CH, CT), F32),
        pltpu.VMEM((NY, CH, 1), F32),
        pltpu.VMEM((NX, NY, CH, FB), BF),
        pltpu.VMEM((2 * NY, CH, RET[0]), BF),
        pltpu.VMEM((2 * NY, 3, CH, RET[0]), BF),
        pltpu.VMEM((2 * NY, NZ, NC, TOK, RET[0]), BF),
        pltpu.VMEM((2 * NY, NZ, TOK, RET[0]), BF),
        pltpu.VMEM((2 * NY - 2, NZ, TOK, RET[0]), BF),
        pltpu.VMEM((2 * NY - 2, NZ, TOK, RET[0]), BF),
        pltpu.VMEM((2, NZ, TOK, RET[0]), F32),
        pltpu.VMEM((2 * NZ - 2, TOK, RET[0]), BF),
        pltpu.VMEM((2 * NZ - 2, TOK, RET[0]), BF),
        pltpu.VMEM((NY, NZ, NC, TOK, FB), BF),
        pltpu.VMEM((PANEL, FB), BF),
        pltpu.VMEM((NY, PANEL, CT), BF),
        pltpu.VMEM((PANEL, FB), F32),
        pltpu.VMEM((PANEL, HID), F32),
        pltpu.VMEM((PANEL, HID), F32),
        pltpu.VMEM((PANEL, PANEL), F32),
        pltpu.VMEM((PANEL, HID), F32),
        pltpu.SemaphoreType.DMA((12,)),
        pltpu.SemaphoreType.DMA((COPIES,)),
        pltpu.SemaphoreType.DMA((COPIES,)),
    ]
    shapes = (
        jax.ShapeDtypeStruct((HID, PANEL), BF),
        jax.ShapeDtypeStruct((TOK, FB), BF),
        jax.ShapeDtypeStruct((BLK, FB), F32),
    )
    results = pl.pallas_call(
        body,
        out_shape=shapes,
        in_specs=[vmem, vmem, vmem, hbm, hbm, hbm, vmem, vmem],
        out_specs=(vmem, vmem, vmem),
        scratch_shapes=scratch,
        compiler_params=pltpu.CompilerParams(
            collective_id=0, has_side_effects=True, vmem_limit_bytes=58 * 1024 * 1024
        ),
        cost_estimate=pl.CostEstimate(flops=6_000_000_000, bytes_accessed=14_000_000, transcendentals=65536),
        name="expert_layer",
    )(tokens, routes.T, probs.T, gate_weight[0], up_weight[0], down_weight[0], masks[0], inv_factor)
    pruned, moe, hessian = pl.pallas_call(
        hand_on,
        out_shape=shapes,
        in_specs=[vmem, vmem, vmem],
        out_specs=(vmem, vmem, vmem),
        name="hand_on",
    )(*results)
    return pruned[None], moe, hessian.T


def solution(mesh):
    in_specs = (
        P("expert", "row"),
        P("expert", None),
        P("expert", None),
        P("expert", "row", None),
        P("expert", "row", None),
        P("expert", "row", None),
        P("expert", "row", None),
        P(),
    )
    out_specs = (P("expert", "row", None), P("expert", "row"), P("row", "expert"))
    return jax.shard_map(
        on_device, mesh=mesh, in_specs=in_specs, out_specs=out_specs, check_vma=False
    )
```

time: 667 us -> 146 us (0.22)
  other arithmetic: 239 us -> 0 us
  waiting for transfers between devices: 168 us -> 0 us
  Pallas kernels: 0 us -> 145 us
  local copies, waits for them, and re-layouts: 133 us -> 0 us
  blocking collectives: 57 us -> 0 us
  matrix products: 32.5 us -> 0 us
  starting transfers between devices: 15.5 us -> 0 us
  between operations: 14.1 us -> 0.64 us
    pallas_call x0 -> x2, Pallas kernels: none -> 145 us  [the longest x1 143 us: on_device(): pl.pallas_call(body, out_shape=shapes, in_specs=[vmem, vmem, vmem, hbm, h...]
    another operation x145 -> x0, other arithmetic: 113 us -> none
    div x128 -> x0, other arithmetic: 108 us -> none  [block_step(): errors_now = (column - kept_vals) / inner_block[column_idx, column_idx]]
    all_gather x1 -> x0, waiting for transfers between devices: 92.9 us -> none  [on_device(): segment = lax.all_gather(full_outputs, 'expert', axis=0, tiled=True)]
    scatter x128 -> x0, local copies, waits for them, and re-layouts: 77 us -> none  [block_step(): segment = segment.at[:, column_idx].set(kept_vals)]
    reduce_scatter x1 -> x0, waiting for transfers between devices: 75.5 us -> none  [on_device(): lax.psum_scatter(lax.dot_general(down_local, hidden, (((0,), (1,)), ((),...]
    all_to_all x1 -> x0, blocking collectives: 36.2 us -> none  [on_device(): lax.all_to_all(expert_outputs, 'expert', split_axis=1, concat_axis=1, til...]
    dot_general x14 -> x0, matrix products: 32.5 us -> none  [the longest x1 11.2 us: on_device(): lax.dot_general(down_local, hidden, (((0,), (1,)), ((), ())), preferred_e...]
  transfers between devices with their start and end apart: 3 -> 0, of which waited for: 2 -> 0; matrix products, arithmetic and copies ran while one was open for 55% -> 0% of each run, Pallas kernels for 0% -> 0%
where the time goes in v1:
time: 146 us
  Pallas kernels  145 us (99%)
    pallas_call x1, Pallas kernels, on_device(): pl.pallas_call(body, out_shape=shapes, in_specs=[vmem, vmem, vmem, hbm, h...  143 us

profile of v1, /device:TPU:1, one launch (start us, length us, event | category | flops | bytes accessed | tf_op | source)
XLA Modules:
  0.0 145.5 jit_solution(17897429907955175841)
XLA Ops:
  0.6 142.7 %expert_layer.1 = (bf16[256,128]{1,0:T(8,128)(2,1)}, bf16[16,1792]{1,0:T(8,128)(2,1)}, f32[112,1792]{1,0:T(8,128)}) custom-call(bf16[16,1792]{1,0:T(8,128)(2,1)} %tokens.1, s32[8,16]{1,0:T(8,128)} %bitcast.14, f32[8,16]{1,0:T(8,128)} %bitcast.15, bf16[256,7168]{1,0:T(8,128)(2,1)} %bitcast.8, bf16[256,7168]{1,0:T(8,128)(2,1)} %bitcast.9, ...), custom_call_target="tpu_custom_call" | custom-call | flops 6000000000 | bytes 14000000 | tf_op jit(solution)/shard_map/expert_layer/pallas_call | solution.py:537
  143.4 2.2 %hand_on.1 = (bf16[256,128]{1,0:T(8,128)(2,1)}, bf16[16,1792]{1,0:T(8,128)(2,1)}, f32[112,1792]{1,0:T(8,128)}) custom-call(bf16[256,128]{1,0:T(8,128)(2,1)} %get-tuple-element.9.pruned, bf16[16,1792]{1,0:T(8,128)(2,1)} %get-tuple-element.10.moe, f32[112,1792]{1,0:T(8,128)} %get-tuple-element.11.hessian), custom_call_target="tpu_custom_call" | custom-call | tf_op jit(solution)/shard_map/hand_on/pallas_call | solution.py:549
